TPU v7x, 32 devices: a whole 2x2x4 slice. The times are simulated.
32 devices in a mesh: parts: 2 (over y), blk: 4 (over z), owner: 2 (over x), sub: 2 (over core).
Axes of the slice: x: 2, y: 2, z: 4, core: 2. Of those that a mesh axis runs over, the one named last changes fastest.
Arguments:
- embeddings: bfloat16 [4096, 512], P(('parts', 'blk', 'owner', 'sub')), parts along dimension 0
- clusters: int32 [4096], P(('parts', 'blk', 'owner', 'sub')), parts along dimension 0, may hold values from 0 to 7
- place: int32 [4096], P(('parts', 'blk', 'owner', 'sub')), parts along dimension 0, may hold values from 0 to 255, as said below
Outputs:
- max_sim: float32 [4096], P(('parts', 'blk', 'owner', 'sub')), parts along dimension 0
There are 2 independent parts, one for each index of `parts`. A program takes and returns all parts, laid end to end along the dimension named above; each array names one. Nothing has to cross between parts.
Inputs may be any that keep to these rules, and one draw needn't show every extreme that they name: place // 32 is a device index along blk and owner together, blk slowest; the places of the rows of one device are distinct; in every draw some destination receives all 32 of its slots from every device of one sub index.
All inputs are finite; a program needn't handle non-finite values.
Results may differ from a plain program's by a relative error of at most 0.00065.
Values may be sent and summed in bfloat16 or wider, within the bound.
A program may use at most 64 MiB of HBM per device.

v0:
```python
import math

import jax
import jax.numpy as jnp
from jax import lax
from jax.sharding import PartitionSpec as P


def pair_scores(mine, other):
    return lax.dot_general(
        mine, other, (((1,), (1,)), ((), ())), preferred_element_type=jnp.float32
    )


def body(embeddings, clusters, place):
    row_count, width = embeddings.shape
    blk_size = lax.axis_size("blk")
    owner_size = lax.axis_size("owner")
    dest_count = blk_size * owner_size
    capacity = 2 * row_count // dest_count
    slot_count = dest_count * capacity
    values = embeddings.astype(jnp.float32)
    scaled = (
        values
        * lax.rsqrt(jnp.mean(values * values, axis=1, keepdims=True) + 1e-06)
        / math.sqrt(width)
    )
    unit_rows = scaled.astype(jnp.bfloat16)
    outgoing = jnp.zeros((slot_count, width), jnp.bfloat16).at[place].set(unit_rows)
    outgoing_ids = jnp.full((slot_count,), -1, jnp.int32).at[place].set(clusters)
    arrived, arrived_ids = (
        lax.all_to_all(outgoing, ("blk", "owner"), split_axis=0, concat_axis=0, tiled=True),
        lax.all_to_all(outgoing_ids, ("blk", "owner"), split_axis=0, concat_axis=0, tiled=True),
    )
    lowest = jnp.full((slot_count,), -1.0, jnp.float32)
    own_start = lax.axis_index("blk") * slot_count
    own_slots = own_start + jnp.arange(slot_count, dtype=jnp.int32)
    piece_rows = lax.all_gather(arrived, "blk", axis=0, tiled=True)
    piece_ids = lax.all_gather(arrived_ids, "blk", axis=0, tiled=True)
    scores = pair_scores(arrived, piece_rows)
    their_slots = jnp.arange(piece_rows.shape[0], dtype=jnp.int32)
    allowed = (arrived_ids[:, None] == piece_ids[None, :]) & (
        own_slots[:, None] != their_slots[None, :]
    )
    best = jnp.maximum(lowest, jnp.max(jnp.where(allowed, scores, -1.0), axis=1))
    answered = lax.all_to_all(best, ("blk", "owner"), split_axis=0, concat_axis=0, tiled=True)
    return jnp.take(answered, place, axis=0)


def solution(mesh):
    in_specs = (
        P(("parts", "blk", "owner", "sub"), None),
        P(("parts", "blk", "owner", "sub")),
        P(("parts", "blk", "owner", "sub")),
    )
    out_specs = P(("parts", "blk", "owner", "sub"))
    return jax.shard_map(body, mesh=mesh, in_specs=in_specs, out_specs=out_specs, check_vma=False)
```

profile of v0, /device:TPU:0, one launch (start us, length us, event | category | flops | bytes accessed | tf_op | source)
XLA Modules:
  0.0 75.7 jit_solution(10477713967849760697)
XLA Ops:
  6.5 0.0 copy-start.1
  6.5 0.0 all-gather.3.cloned.1.call-start
  6.5 0.7 compare_select_fusion
  7.2 1.0 %fusion.2 = f32[128]{0:T(128)S(1)} fusion(bf16[128,512]{1,0:T(8,128)(2,1)} %param.3), kind=kLoop, calls=%fused_computation.9 | loop fusion | flops 196480 | bytes 131584 | tf_op jit(solution)/shard_map/reduce_sum | solution.py:25
  8.3 0.0 copy-done.1
  8.3 1.2 %scatter_custom_fusion.1 = bf16[256,512]{1,0:T(8,128)(2,1)S(1)} fusion(s32[128]{0:T(128)S(1)} %compare_select_fusion, bf16[128,512]{1,0:T(8,128)(2,1)S(1)} %copy-done.1, f32[]{:T(128)} %constant.39.clone.1, f32[128]{0:T(128)S(1)} %add_rsqrt_fusion, bf16[]{:T(256)} %constant.11.clone.1), kind=kCustom, calls=%fused_computation.12 | custom fusion | flops 262144 | bytes 393734 | tf_op jit(solution)/shard_map/scatter | solution.py:29
  9.5 16.1 %all_to_all.30 = bf16[8,32,512]{2,1,0:T(8,128)(2,1)} all-to-all(bf16[8,32,512]{2,1,0:T(8,128)(2,1)S(1)} %bitcast.14), channel_id=1, replica_groups=mesh['parts'=2,'blk'=4,'owner'=2,'sub'=2] {'blk','owner'}, dimensions={0} | all-to-all | bytes 524288 | tf_op jit(solution)/shard_map/all_to_all | solution.py:32
  25.6 0.0 copy-start
  25.6 0.0 all-gather.3.cloned.1.call-update
  25.6 1.2 %scatter_custom_fusion = s32[256]{0:T(256)S(1)} fusion(s32[128]{0:T(128)S(1)} %compare_select_fusion, s32[128]{0:T(128)} %param.4, s32[]{:T(128)} %constant.17.clone.1), kind=kCustom, calls=%fused_computation.22 | custom fusion | bytes 1536 | tf_op jit(solution)/shard_map/scatter | solution.py:30
  26.8 0.7 all_to_all.20
  27.5 3.6 %all-to-all-start = ((s32[8,32,1]{1,2,0:T(1,128)}), s32[8,32,1]{1,2,0:T(1,128)S(1)}, u32[]{:S(2)}, u32[]{:S(2)}) async-start(s32[8,32,1]{1,2,0:T(1,128)} %bitcast), calls=%async_computation | async-start | bytes 8192 | tf_op jit(solution)/shard_map/all_to_all | solution.py:33
  31.1 6.6 %all-to-all-done = s32[8,32,1]{1,2,0:T(1,128)S(1)} async-done(((s32[8,32,1]{1,2,0:T(1,128)}), s32[8,32,1]{1,2,0:T(1,128)S(1)}, u32[]{:S(2)}, u32[]{:S(2)}) %all-to-all-start) | async-done | bytes 1056 | tf_op jit(solution)/shard_map/all_to_all | solution.py:33
  37.6 0.1 reshape.65
  37.7 0.5 broadcast.42
  38.2 0.7 reduce.8
  38.9 0.1 eq.15
  39.0 8.1 %all-gather = s32[4,1,256]{2,1,0:T(1,128)S(1)} all-gather(s32[1,1,256]{2,1,0:T(1,128)S(1)} %reshape.65), channel_id=1, replica_groups=mesh['parts'=2,'blk'=4,'owner'=2,'sub'=2] {'blk'}, dimensions={0}, use_global_device_ids=true | all-gather | bytes 5120 | tf_op jit(solution)/shard_map/all_gather | solution.py:39
  47.1 5.7 %all-gather.3.cloned.1.call-done = bf16[1024,512]{1,0:T(8,128)(2,1)} async-done(((bf16[256,512]{1,0:T(8,128)(2,1)}), bf16[1024,512]{1,0:T(8,128)(2,1)}) %all-gather.3.cloned.1.call-update) | async-done | bytes 1048592 | tf_op jit(solution)/shard_map/all_gather | solution.py:38
  52.8 0.0 copy-done
  52.8 1.8 %fusion = f32[256]{0:T(256)S(1)} fusion(bf16[256,512]{1,0:T(8,128)(2,1)S(1)} %bitcast.13, bf16[1024,512]{1,0:T(8,128)(2,1)} %all-gather.3.cloned.1.call-done, s32[256]{0:T(256)S(1)} %iota_add_fusion, s32[1024]{0:T(1024)S(1)} %bitcast.16, s32[256]{0:T(256)S(1)} %eq.15), kind=kOutput, calls=%fused_computation.4 | convolution fusion | flops 269745920 | bytes 1317888 | tf_op jit(solution)/shard_map/dot_general | solution.py:10
  54.6 0.7 max_broadcast_in_dim.14
  55.3 4.0 %all-to-all-start.2 = ((f32[8,32,1]{1,2,0:T(1,128)}), f32[8,32,1]{1,2,0:T(1,128)S(1)}, u32[]{:S(2)}, u32[]{:S(2)}) async-start(f32[8,32,1]{1,2,0:T(1,128)} %bitcast.4), calls=%async_computation.2 | async-start | bytes 8192 | tf_op jit(solution)/shard_map/all_to_all | solution.py:46
  59.4 6.5 %all-to-all-done.2 = f32[8,32,1]{1,2,0:T(1,128)S(1)} async-done(((f32[8,32,1]{1,2,0:T(1,128)}), f32[8,32,1]{1,2,0:T(1,128)S(1)}, u32[]{:S(2)}, u32[]{:S(2)}) %all-to-all-start.2) | async-done | bytes 1056 | tf_op jit(solution)/shard_map/all_to_all | solution.py:46
  65.8 0.5 broadcast.43
  66.3 0.7 reduce.9
  67.0 0.1 all_to_all.26
  67.1 0.0 copy-start.2
  67.1 1.3 %gather_fusion = f32[128]{0:T(128)S(1)} fusion(f32[256]{0:T(256)S(1)} %all_to_all.26, s32[1024]{0:T(1024)S(1)} %pad_clamp_fusion), kind=kCustom, calls=%fused_computation | custom fusion | bytes 1536 | tf_op jit(solution)/shard_map/jit(_take)/gather | solution.py:47
  68.4 0.0 copy-done.2
  68.4 0.5 and_select_fusion
  (4 shorter events, 0.0 us)
Async XLA Ops:
  6.5 1.7 %copy-start.1 = (bf16[128,512]{1,0:T(8,128)(2,1)S(1)}, bf16[128,512]{1,0:T(8,128)(2,1)}, u32[]{:S(2)}) copy-start(bf16[128,512]{1,0:T(8,128)(2,1)} %param.3) | copy-start | bytes 393220
  6.5 46.3 %all-gather.3.cloned.1.call-start = ((), (), s32[]{:S(2)}) async-start(), calls=%async_computation.3 | async-start | bytes 1310720 | tf_op jit(solution)/shard_map/all_gather | solution.py:38
  25.6 27.3 %copy-start = (bf16[8,32,512]{2,1,0:T(8,128)(2,1)S(1)}, bf16[8,32,512]{2,1,0:T(8,128)(2,1)}, u32[]{:S(2)}) copy-start(bf16[8,32,512]{2,1,0:T(8,128)(2,1)} %all_to_all.30) | copy-start | bytes 786436
  27.5 10.2 %all-to-all-start = ((s32[8,32,1]{1,2,0:T(1,128)}), s32[8,32,1]{1,2,0:T(1,128)S(1)}, u32[]{:S(2)}, u32[]{:S(2)}) async-start(s32[8,32,1]{1,2,0:T(1,128)} %bitcast), calls=%async_computation | async-start | bytes 8192 | tf_op jit(solution)/shard_map/all_to_all | solution.py:33
  55.3 10.5 %all-to-all-start.2 = ((f32[8,32,1]{1,2,0:T(1,128)}), f32[8,32,1]{1,2,0:T(1,128)S(1)}, u32[]{:S(2)}, u32[]{:S(2)}) async-start(f32[8,32,1]{1,2,0:T(1,128)} %bitcast.4), calls=%async_computation.2 | async-start | bytes 8192 | tf_op jit(solution)/shard_map/all_to_all | solution.py:46
  67.1 1.3 %copy-start.2 = (s32[128]{0:T(128)S(1)}, s32[128]{0:T(128)}, u32[]{:S(2)}) copy-start(s32[128]{0:T(128)} %param.5) | copy-start | bytes 1540
Sparse Core Ops, SparseCore 0:
  25.7 27.0 all-gather.2
where the time goes:
time: 76.1 us; the launch traced here: 75.7 us
  blocking collectives  24.2 us (32%)
  waiting for transfers between devices  18.7 us (25%)
  between operations  13.5 us (18%)
  starting transfers between devices  7.63 us (10%)
  local copies, waits for them, and re-layouts  5.12 us (7%)
  other arithmetic  4.76 us (6%)
  matrix products  1.83 us (2%)
    all_to_all x1, blocking collectives, body(): lax.all_to_all(outgoing, ('blk', 'owner'), split_axis=0, concat_axis=0, t...  16.1 us
    all_gather x1, blocking collectives, body(): piece_ids = lax.all_gather(arrived_ids, 'blk', axis=0, tiled=True)  8.13 us
    all_to_all x1, waiting for transfers between devices, body(): lax.all_to_all(outgoing_ids, ('blk', 'owner'), split_axis=0, concat_axis=...  6.56 us
    all_to_all x1, waiting for transfers between devices, body(): lax.all_to_all(best, ('blk', 'owner'), split_axis=0, concat_axis=0, tiled...  6.46 us
    all_gather x1, waiting for transfers between devices, body(): piece_rows = lax.all_gather(arrived, 'blk', axis=0, tiled=True)  5.7 us
    all_to_all x1, starting transfers between devices, body(): lax.all_to_all(best, ('blk', 'owner'), split_axis=0, concat_axis=0, tiled...  4.04 us
    all_to_all x1, starting transfers between devices, body(): lax.all_to_all(outgoing_ids, ('blk', 'owner'), split_axis=0, concat_axis=...  3.59 us
    dot_general x1, matrix products, pair_scores(): lax.dot_general(mine, other, (((1,), (1,)), ((), ())), preferred_element_...  1.83 us
  transfers between devices with their start and end apart: 3, of which 3 were waited for; matrix products, arithmetic and copies ran while one was open for 3% of the time, Pallas kernels for 0%

commit v1 on v0

v1 whole, which is shorter than its diff:
```python
import functools
import math

import jax
import jax.numpy as jnp
from jax import lax
from jax.experimental import pallas as pl
from jax.experimental.pallas import tpu as pltpu
from jax.sharding import PartitionSpec as P

MESH = pl.DeviceIdType.MESH
LOWEST = -1.0


def each(start, stop, step):
    if stop - start <= 8:
        for index in range(start, stop):
            step(index)
    else:
        lax.fori_loop(start, stop, lambda index, _: (step(index), 0)[1], 0)


def pair_scores(mine, other):
    return lax.dot_general(
        mine, other, (((1,), (1,)), ((), ())), preferred_element_type=jnp.float32
    )


def div_rem(values, cap, n_own):
    return lax.rem(lax.div(values, jnp.int32(cap)), jnp.int32(n_own))


def kernel(
    n_blk, n_own, cap,
    emb_ref, clusters_ref, place_ref, out_ref,
    emb, rows, row_keys, cols, col_keys, best,
    col_answer, col_back, row_answer, row_back,
    load_sem, col_send, col_recv, row_send, row_recv,
    col_back_send, col_back_recv, row_back_send, row_back_recv,
):
    n_rows, width = emb.shape
    z = lax.axis_index("blk")
    x = lax.axis_index("owner")
    sub = lax.axis_index("sub")
    pos = jnp.where(sub == 0, z, n_blk - 1 - z)
    sign = 1 - 2 * sub

    load = pltpu.make_async_copy(emb_ref, emb, load_sem)
    load.start()

    barrier = pltpu.get_barrier_semaphore()
    each(1, n_own, lambda e: pl.semaphore_signal(
        barrier, inc=1, device_id={"owner": lax.rem(x + e, n_own)}, device_id_type=MESH))
    each(1, n_blk, lambda d: pl.semaphore_signal(
        barrier, inc=1, device_id={"blk": lax.rem(z + d, n_blk)}, device_id_type=MESH))

    def col_copies(d):
        target = {"blk": jnp.clip(z + sign * d, 0, n_blk - 1)}
        return [
            pltpu.make_async_remote_copy(
                src_ref=src, dst_ref=dst, send_sem=col_send.at[d, k], recv_sem=col_recv.at[d, k],
                device_id=target, device_id_type=MESH)
            for k, (src, dst) in enumerate((
                (row_keys.at[0], col_keys.at[d]), (rows.at[pl.ds(0, n_rows)], cols.at[d])))
        ]

    def row_copies(e):
        target = {"owner": lax.rem(x + e, n_own)}
        return [
            pltpu.make_async_remote_copy(
                src_ref=src, dst_ref=dst, send_sem=row_send.at[e, k], recv_sem=row_recv.at[e, k],
                device_id=target, device_id_type=MESH)
            for k, (src, dst) in enumerate((
                (row_keys.at[0], row_keys.at[e]),
                (rows.at[pl.ds(0, n_rows)], rows.at[pl.ds(e * n_rows, n_rows)])))
        ]

    def col_return(d):
        return pltpu.make_async_remote_copy(
            src_ref=col_answer.at[d], dst_ref=col_back.at[d],
            send_sem=col_back_send.at[d], recv_sem=col_back_recv.at[d],
            device_id={"blk": jnp.clip(z - sign * d, 0, n_blk - 1)}, device_id_type=MESH)

    def row_return(e):
        return pltpu.make_async_remote_copy(
            src_ref=row_answer.at[e], dst_ref=row_back.at[e],
            send_sem=row_back_send.at[e], recv_sem=row_back_recv.at[e],
            device_id={"owner": lax.rem(x + n_own - e, n_own)}, device_id_type=MESH)

    group = div_rem(place_ref[...], cap, n_own)
    my_key = group * 65536 + clusters_ref[...]
    row_keys[0] = my_key
    load.wait()
    values = emb[...].astype(jnp.float32)
    mean = jnp.mean(values * values, axis=1, keepdims=True)
    unit = values * (lax.rsqrt(mean + 1e-06) * (1.0 / math.sqrt(width)))
    rows[pl.ds(0, n_rows)] = unit.astype(jnp.bfloat16)

    pl.semaphore_wait(barrier, n_blk - 1 + n_own - 1)

    def send_cols(d):
        @pl.when(pos + d < n_blk)
        def _():
            for copy in col_copies(d):
                copy.start()

    each(1, n_blk, send_cols)

    def send_rows(e):
        for copy in row_copies(e):
            copy.start()

    each(1, n_own, send_rows)

    def down(key):
        return jnp.transpose(jnp.broadcast_to(key, (n_rows, n_rows)))

    my_down = down(my_key)
    mine = rows[pl.ds(0, n_rows)]
    shape = (n_rows, n_rows)
    other = lax.broadcasted_iota(jnp.int32, shape, 0) != lax.broadcasted_iota(jnp.int32, shape, 1)
    best[pl.ds(0, n_rows)] = jnp.where(
        (my_down == my_key) & other, pair_scores(mine, mine), LOWEST)

    def meet_row(e):
        for copy in row_copies(e):
            copy.wait_recv()
        theirs = rows[pl.ds(e * n_rows, n_rows)]
        found = jnp.where(my_down == row_keys[e], pair_scores(mine, theirs), LOWEST)
        best[pl.ds(0, n_rows)] = jnp.maximum(best[pl.ds(0, n_rows)], found)
        best[pl.ds(e * n_rows, n_rows)] = jnp.full(shape, LOWEST, jnp.float32)

    each(1, n_own, meet_row)

    def meet_col(d):
        @pl.when(pos >= d)
        def _():
            for copy in col_copies(d):
                copy.wait_recv()
            col_key = col_keys[d]
            scores = pair_scores(rows[...], cols[d])
            answer = None
            for e in range(n_own):
                here = pl.ds(e * n_rows, n_rows)
                found = jnp.where(
                    down(row_keys[e]) == col_key, scores[e * n_rows:(e + 1) * n_rows], LOWEST)
                best[here] = jnp.maximum(best[here], found)
                top = jnp.max(found, axis=0, keepdims=True)
                answer = top if answer is None else jnp.maximum(answer, top)
            col_answer[d] = answer
            col_return(d).start()

    each(1, n_blk, meet_col)

    def answer_row(e):
        @pl.when(pos > 0)
        def _():
            row_answer[e] = jnp.max(
                jnp.transpose(best[pl.ds(e * n_rows, n_rows)]), axis=0, keepdims=True)
            row_return(e).start()

    each(1, n_own, answer_row)

    out_ref[...] = jnp.max(jnp.transpose(best[pl.ds(0, n_rows)]), axis=0, keepdims=True)

    def take_row(e):
        for copy in row_copies(e):
            copy.wait_send()

        @pl.when(pos > 0)
        def _():
            row_return(e).wait()
            out_ref[...] = jnp.maximum(out_ref[...], row_back[e])

    def take_col(d):
        @pl.when(pos + d < n_blk)
        def _():
            for copy in col_copies(d):
                copy.wait_send()
            col_return(d).wait_recv()
            out_ref[...] = jnp.maximum(out_ref[...], col_back[d])

        @pl.when(pos >= d)
        def _():
            col_return(d).wait_send()

    each(1, n_own, take_row)
    each(1, n_blk, take_col)


def body(embeddings, clusters, place):
    n_rows, width = embeddings.shape
    n_blk = lax.axis_size("blk")
    n_own = lax.axis_size("owner")
    cap = 2 * n_rows // (n_blk * n_own)
    vmem = pl.BlockSpec(memory_space=pltpu.VMEM)
    dma = pltpu.SemaphoreType.DMA
    best = pl.pallas_call(
        functools.partial(kernel, n_blk, n_own, cap),
        out_shape=jax.ShapeDtypeStruct((1, n_rows), jnp.float32),
        in_specs=[pl.BlockSpec(memory_space=pl.ANY), vmem, vmem],
        out_specs=vmem,
        scratch_shapes=[
            pltpu.VMEM((n_rows, width), jnp.bfloat16),
            pltpu.VMEM((n_own * n_rows, width), jnp.bfloat16),
            pltpu.VMEM((n_own, 1, n_rows), jnp.int32),
            pltpu.VMEM((n_blk, n_rows, width), jnp.bfloat16),
            pltpu.VMEM((n_blk, 1, n_rows), jnp.int32),
            pltpu.VMEM((n_own * n_rows, n_rows), jnp.float32),
            pltpu.VMEM((n_blk, 1, n_rows), jnp.float32),
            pltpu.VMEM((n_blk, 1, n_rows), jnp.float32),
            pltpu.VMEM((n_own, 1, n_rows), jnp.float32),
            pltpu.VMEM((n_own, 1, n_rows), jnp.float32),
            dma,
            dma((n_blk, 2)), dma((n_blk, 2)), dma((n_own, 2)), dma((n_own, 2)),
            dma((n_blk,)), dma((n_blk,)), dma((n_own,)), dma((n_own,)),
        ],
        compiler_params=pltpu.CompilerParams(collective_id=0, has_side_effects=True),
    )(embeddings, clusters.reshape(1, n_rows), place.reshape(1, n_rows))
    return best.reshape(n_rows)


def solution(mesh):
    spread = ("parts", "blk", "owner", "sub")
    return jax.shard_map(
        body, mesh=mesh, in_specs=(P(spread, None), P(spread), P(spread)), out_specs=P(spread),
        check_vma=False)
```

time: 76.1 us -> 20 us (0.26)
  blocking collectives: 24.2 us -> 0 us
  Pallas kernels: 0 us -> 18.7 us
  waiting for transfers between devices: 18.7 us -> 0 us
  between operations: 13.5 us -> 0.02 us
  starting transfers between devices: 7.63 us -> 0 us
  other arithmetic: 4.76 us -> 0 us
  local copies, waits for them, and re-layouts: 5.12 us -> 1.1 us
  matrix products: 1.83 us -> 0 us
    pallas_call x0 -> x1, Pallas kernels: none -> 18.7 us  [body(): pl.pallas_call(functools.partial(kernel, n_blk, n_own, cap), out_shape=ja...]
    all_to_all x1 -> x0, blocking collectives: 16.1 us -> none  [body(): lax.all_to_all(outgoing, ('blk', 'owner'), split_axis=0, concat_axis=0, t...]
    all_to_all x2 -> x0, waiting for transfers between devices: 13 us -> none  [the longest x1 6.56 us: body(): lax.all_to_all(outgoing_ids, ('blk', 'owner'), split_axis=0, concat_axis=...]
    all_gather x1 -> x0, blocking collectives: 8.13 us -> none  [body(): piece_ids = lax.all_gather(arrived_ids, 'blk', axis=0, tiled=True)]
    all_to_all x2 -> x0, starting transfers between devices: 7.62 us -> none  [the longest x1 4.04 us: body(): lax.all_to_all(best, ('blk', 'owner'), split_axis=0, concat_axis=0, tiled...]
    all_gather x1 -> x0, waiting for transfers between devices: 5.7 us -> none  [body(): piece_rows = lax.all_gather(arrived, 'blk', axis=0, tiled=True)]
    dot_general x1 -> x0, matrix products: 1.83 us -> none  [pair_scores(): lax.dot_general(mine, other, (((1,), (1,)), ((), ())), preferred_element_...]
    all_to_all x4 -> x0, local copies, waits for them, and re-layouts: 1.77 us -> none  [the longest x2 1.18 us: body(): lax.all_to_all(outgoing_ids, ('blk', 'owner'), split_axis=0, concat_axis=...]
  transfers between devices with their start and end apart: 3 -> 0, of which waited for: 3 -> 0; matrix products, arithmetic and copies ran while one was open for 3% -> 0% of each run, Pallas kernels for 0% -> 0%
where the time goes in v1:
time: 20 us; the launch traced here: 19.8 us
  Pallas kernels  18.7 us (94%)
  local copies, waits for them, and re-layouts  1.1 us (6%)
    pallas_call x1, Pallas kernels, body(): pl.pallas_call(functools.partial(kernel, n_blk, n_own, cap), out_shape=ja...  18.7 us
    unnamed x3, local copies, waits for them, and re-layouts  1.1 us

profile of v1, /device:TPU:0, one launch (start us, length us, event | category | flops | bytes accessed | tf_op | source)
XLA Modules:
  0.0 19.8 jit_solution(10591029898787445729)
XLA Ops:
  0.0 18.7 %shard_map.37 = f32[1,128]{1,0:T(1,128)} custom-call(bf16[128,512]{1,0:T(8,128)(2,1)} %emb_ref.1, s32[1,128]{1,0:T(1,128)} %bitcast.3, s32[1,128]{1,0:T(1,128)} %bitcast.4), custom_call_target="tpu_custom_call" | custom-call | tf_op jit(solution)/shard_map/pallas_call | solution.py:198
  18.7 0.0 copy-start
  18.7 0.6 %copy-done = f32[1,128]{1,0:T(1,128)S(1)} copy-done((f32[1,128]{1,0:T(1,128)S(1)}, f32[1,128]{1,0:T(1,128)}, u32[]{:S(2)}) %copy-start) | copy-done | bytes 536
  19.3 0.5 %copy.5 = f32[128]{0:T(128)} copy(f32[128]{0:T(128)S(1)} %bitcast.5) | data formatting | bytes 1024
Async XLA Ops:
  18.7 0.6 %copy-start = (f32[1,128]{1,0:T(1,128)S(1)}, f32[1,128]{1,0:T(1,128)}, u32[]{:S(2)}) copy-start(f32[1,128]{1,0:T(1,128)} %shard_map.37) | copy-start | bytes 1540

commit v2 on v1

v2 whole, which is shorter than its diff:
```python
import functools
import math

import jax
import jax.numpy as jnp
from jax import lax
from jax.experimental import pallas as pl
from jax.experimental.pallas import tpu as pltpu
from jax.sharding import PartitionSpec as P

MESH = pl.DeviceIdType.MESH
LOWEST = -1.0


def each(start, stop, step):
    if stop - start <= 8:
        for index in range(start, stop):
            step(index)
    else:
        lax.fori_loop(start, stop, lambda index, _: (step(index), 0)[1], 0)


def pair_scores(mine, other):
    return lax.dot_general(
        mine, other, (((1,), (1,)), ((), ())), preferred_element_type=jnp.float32
    )


def div_rem(values, cap, n_own):
    return lax.rem(lax.div(values, jnp.int32(cap)), jnp.int32(n_own))


def kernel(
    n_blk, n_own, cap,
    emb_ref, clusters_ref, place_ref, out_ref,
    emb, clusters, place, rows, row_keys, cols, col_keys, best, down_keys,
    col_answer, col_back, row_answer, row_back,
    load_sem, col_send, col_recv, row_send, row_recv,
    col_back_send, col_back_recv, row_back_send, row_back_recv,
):
    n_rows, width = emb.shape
    z = lax.axis_index("blk")
    x = lax.axis_index("owner")
    sub = lax.axis_index("sub")

    def flows(a, b):
        low, apart = jnp.minimum(a, b), jnp.abs(a - b)
        up = (apart < n_blk - 1) & ((sub == 1) | (low == apart - 1))
        return ((a < b) & up) | ((a > b) & ~up)

    loads = [
        pltpu.make_async_copy(src, dst, load_sem.at[k])
        for k, (src, dst) in enumerate((
            (emb_ref, emb), (clusters_ref, clusters), (place_ref, place)))
    ]
    for load in loads:
        load.start()

    barrier = pltpu.get_barrier_semaphore()
    each(1, n_own, lambda e: pl.semaphore_signal(
        barrier, inc=1, device_id={"owner": lax.rem(x + e, n_own)}, device_id_type=MESH))

    def greet(a):
        @pl.when(flows(a, z))
        def _():
            pl.semaphore_signal(barrier, inc=1, device_id={"blk": a}, device_id_type=MESH)

    each(0, n_blk, greet)

    def col_copies(a, b):
        return [
            pltpu.make_async_remote_copy(
                src_ref=src, dst_ref=dst, send_sem=col_send.at[b, k], recv_sem=col_recv.at[a, k],
                device_id={"blk": b}, device_id_type=MESH)
            for k, (src, dst) in enumerate((
                (row_keys.at[0], col_keys.at[a]), (rows.at[pl.ds(0, n_rows)], cols.at[a])))
        ]

    def row_copies(e):
        target = {"owner": lax.rem(x + e, n_own)}
        return [
            pltpu.make_async_remote_copy(
                src_ref=src, dst_ref=dst, send_sem=row_send.at[e, k], recv_sem=row_recv.at[e, k],
                device_id=target, device_id_type=MESH)
            for k, (src, dst) in enumerate((
                (row_keys.at[0], row_keys.at[e]),
                (rows.at[pl.ds(0, n_rows)], rows.at[pl.ds(e * n_rows, n_rows)])))
        ]

    def col_return(a, b):
        return pltpu.make_async_remote_copy(
            src_ref=col_answer.at[a], dst_ref=col_back.at[b],
            send_sem=col_back_send.at[a], recv_sem=col_back_recv.at[b],
            device_id={"blk": a}, device_id_type=MESH)

    def row_return(e):
        return pltpu.make_async_remote_copy(
            src_ref=row_answer.at[e], dst_ref=row_back.at[e],
            send_sem=row_back_send.at[e], recv_sem=row_back_recv.at[e],
            device_id={"owner": lax.rem(x + n_own - e, n_own)}, device_id_type=MESH)

    def down(key):
        return jnp.transpose(jnp.broadcast_to(key, (n_rows, n_rows)))

    for load in loads:
        load.wait()
    group = div_rem(place[...], cap, n_own)
    my_key = group * 65536 + clusters[...]
    row_keys[0] = my_key
    values = emb[...].astype(jnp.float32)
    mean = jnp.mean(values * values, axis=1, keepdims=True)
    unit = values * (lax.rsqrt(mean + 1e-06) * (1.0 / math.sqrt(width)))
    rows[pl.ds(0, n_rows)] = unit.astype(jnp.bfloat16)

    targets = sum(flows(z, b).astype(jnp.int32) for b in range(n_blk))
    pl.semaphore_wait(barrier, targets + n_own - 1)

    def send_cols(b):
        @pl.when(flows(z, b))
        def _():
            for copy in col_copies(z, b):
                copy.start()

    each(0, n_blk, send_cols)

    def send_rows(e):
        for copy in row_copies(e):
            copy.start()

    each(1, n_own, send_rows)

    down_keys[pl.ds(0, n_rows)] = down(my_key)
    mine = rows[pl.ds(0, n_rows)]
    shape = (n_rows, n_rows)
    other = lax.broadcasted_iota(jnp.int32, shape, 0) != lax.broadcasted_iota(jnp.int32, shape, 1)
    best[pl.ds(0, n_rows)] = jnp.where(
        (down_keys[pl.ds(0, n_rows)] == my_key) & other, pair_scores(mine, mine), LOWEST)

    def meet_row(e):
        for copy in row_copies(e):
            copy.wait_recv()
        theirs = rows[pl.ds(e * n_rows, n_rows)]
        down_keys[pl.ds(e * n_rows, n_rows)] = down(row_keys[e])
        found = jnp.where(
            down_keys[pl.ds(0, n_rows)] == row_keys[e], pair_scores(mine, theirs), LOWEST)
        best[pl.ds(0, n_rows)] = jnp.maximum(best[pl.ds(0, n_rows)], found)
        best[pl.ds(e * n_rows, n_rows)] = jnp.full(shape, LOWEST, jnp.float32)

    each(1, n_own, meet_row)

    def meet_col(a):
        @pl.when(flows(a, z))
        def _():
            for copy in col_copies(a, z):
                copy.wait_recv()
            col_key = col_keys[a]
            scores = pair_scores(rows[...], cols[a])
            answer = None
            for e in range(n_own):
                here = pl.ds(e * n_rows, n_rows)
                found = jnp.where(
                    down_keys[here] == col_key, scores[e * n_rows:(e + 1) * n_rows], LOWEST)
                best[here] = jnp.maximum(best[here], found)
                top = jnp.max(found, axis=0, keepdims=True)
                answer = top if answer is None else jnp.maximum(answer, top)
            col_answer[a] = answer
            col_return(a, z).start()

    each(0, n_blk, meet_col)

    def answer_row(e):
        row_answer[e] = jnp.max(
            jnp.transpose(best[pl.ds(e * n_rows, n_rows)]), axis=0, keepdims=True)
        row_return(e).start()

    each(1, n_own, answer_row)

    out_ref[...] = jnp.max(jnp.transpose(best[pl.ds(0, n_rows)]), axis=0, keepdims=True)

    def take_col(b):
        @pl.when(flows(z, b))
        def _():
            for copy in col_copies(z, b):
                copy.wait_send()
            col_return(z, b).wait_recv()
            out_ref[...] = jnp.maximum(out_ref[...], col_back[b])

        @pl.when(flows(b, z))
        def _():
            col_return(b, z).wait_send()

    def take_row(e):
        for copy in row_copies(e):
            copy.wait_send()
        row_return(e).wait()
        out_ref[...] = jnp.maximum(out_ref[...], row_back[e])

    each(0, n_blk, take_col)
    each(1, n_own, take_row)


def body(embeddings, clusters, place):
    n_rows, width = embeddings.shape
    n_blk = lax.axis_size("blk")
    n_own = lax.axis_size("owner")
    cap = 2 * n_rows // (n_blk * n_own)
    vmem = pl.BlockSpec(memory_space=pltpu.VMEM)
    dma = pltpu.SemaphoreType.DMA
    best = pl.pallas_call(
        functools.partial(kernel, n_blk, n_own, cap),
        out_shape=pltpu.VMEM((1, n_rows), jnp.float32),
        in_specs=[pl.BlockSpec(memory_space=pltpu.HBM)] * 3,
        out_specs=vmem,
        scratch_shapes=[
            pltpu.VMEM((n_rows, width), jnp.bfloat16),
            pltpu.VMEM((1, n_rows), jnp.int32),
            pltpu.VMEM((1, n_rows), jnp.int32),
            pltpu.VMEM((n_own * n_rows, width), jnp.bfloat16),
            pltpu.VMEM((n_own, 1, n_rows), jnp.int32),
            pltpu.VMEM((n_blk, n_rows, width), jnp.bfloat16),
            pltpu.VMEM((n_blk, 1, n_rows), jnp.int32),
            pltpu.VMEM((n_own * n_rows, n_rows), jnp.float32),
            pltpu.VMEM((n_own * n_rows, n_rows), jnp.int32),
            pltpu.VMEM((n_blk, 1, n_rows), jnp.float32),
            pltpu.VMEM((n_blk, 1, n_rows), jnp.float32),
            pltpu.VMEM((n_own, 1, n_rows), jnp.float32),
            pltpu.VMEM((n_own, 1, n_rows), jnp.float32),
            dma((3,)),
            dma((n_blk, 2)), dma((n_blk, 2)), dma((n_own, 2)), dma((n_own, 2)),
            dma((n_blk,)), dma((n_blk,)), dma((n_own,)), dma((n_own,)),
        ],
        compiler_params=pltpu.CompilerParams(collective_id=0, has_side_effects=True),
    )(embeddings, clusters.reshape(1, n_rows), place.reshape(1, n_rows))
    return best.reshape(n_rows)


def solution(mesh):
    spread = ("parts", "blk", "owner", "sub")
    return jax.shard_map(
        body, mesh=mesh, in_specs=(P(spread, None), P(spread), P(spread)), out_specs=P(spread),
        check_vma=False)
```

time: 20 us -> 15.4 us (0.77)
  Pallas kernels: 18.7 us -> 14.8 us
  local copies, waits for them, and re-layouts: 1.1 us -> 0.51 us
    pallas_call x1, Pallas kernels: 18.7 us -> 14.8 us  [body(): pl.pallas_call(functools.partial(kernel, n_blk, n_own, cap), out_shape=pl...]
    unnamed x3 -> x1, local copies, waits for them, and re-layouts: 1.1 us -> 0.51 us
where the time goes in v2:
time: 15.4 us; the launch traced here: 15.3 us
  Pallas kernels  14.8 us (96%)
  local copies, waits for them, and re-layouts  0.51 us (3%)
    pallas_call x1, Pallas kernels, body(): pl.pallas_call(functools.partial(kernel, n_blk, n_own, cap), out_shape=pl...  14.8 us
    unnamed x1, local copies, waits for them, and re-layouts  0.51 us

profile of v2, /device:TPU:0, one launch (start us, length us, event | category | flops | bytes accessed | tf_op | source)
XLA Modules:
  0.0 15.3 jit_solution(15938314372636440200)
XLA Ops:
  0.0 14.8 %shard_map.37 = f32[1,128]{1,0:T(1,128)S(1)} custom-call(bf16[128,512]{1,0:T(8,128)(2,1)} %emb_ref.1, s32[1,128]{1,0:T(1,128)} %bitcast.4, s32[1,128]{1,0:T(1,128)} %bitcast.5), custom_call_target="tpu_custom_call" | custom-call | tf_op jit(solution)/shard_map/pallas_call | solution.py:209
  14.8 0.5 %copy.5 = f32[128]{0:T(128)} copy(f32[128]{0:T(128)S(1)} %bitcast.3) | data formatting | bytes 1024

commit v3 on v2

v3 whole, which is shorter than its diff:
```python
import functools
import math

import jax
import jax.numpy as jnp
from jax import lax
from jax.experimental import pallas as pl
from jax.experimental.pallas import tpu as pltpu
from jax.sharding import PartitionSpec as P

MESH = pl.DeviceIdType.MESH
LOWEST = -1.0


def each(start, stop, step):
    if stop - start <= 8:
        for index in range(start, stop):
            step(index)
    else:
        lax.fori_loop(start, stop, lambda index, _: (step(index), 0)[1], 0)


def pair_scores(mine, other):
    return lax.dot_general(
        mine, other, (((1,), (1,)), ((), ())), preferred_element_type=jnp.float32
    )


def div_rem(values, cap, n_own):
    return lax.rem(lax.div(values, jnp.int32(cap)), jnp.int32(n_own))


def kernel(
    n_blk, n_own, cap,
    emb_ref, clusters_ref, place_ref, out_ref,
    emb, rows, row_keys, cols, col_keys, answer,
    col_answer, col_back, row_back,
    load_sem, col_send, col_recv, row_send, row_recv,
    col_back_send, col_back_recv, row_back_send, row_back_recv,
):
    n_rows, width = emb.shape
    z = lax.axis_index("blk")
    x = lax.axis_index("owner")
    sub = lax.axis_index("sub")

    def flows(a, b):
        low, apart = jnp.minimum(a, b), jnp.abs(a - b)
        up = (apart < n_blk - 1) & ((sub == 0) | ((low == 1) & (apart == 1)))
        return ((a < b) & up) | ((a > b) & ~up)

    loads = [
        pltpu.make_async_copy(src, dst, load_sem.at[k])
        for k, (src, dst) in enumerate((
            (emb_ref, emb), (clusters_ref, row_keys.at[0, 0]), (place_ref, row_keys.at[0, 1])))
    ]
    for load in loads:
        load.start()

    barrier = pltpu.get_barrier_semaphore()
    each(1, n_own, lambda e: pl.semaphore_signal(
        barrier, inc=1, device_id={"owner": lax.rem(x + e, n_own)}, device_id_type=MESH))

    def greet(a):
        @pl.when(flows(a, z))
        def _():
            pl.semaphore_signal(barrier, inc=1, device_id={"blk": a}, device_id_type=MESH)

    each(0, n_blk, greet)

    def col_copy(a, b, k):
        src, dst = (
            (clusters_ref, col_keys.at[a, 0]), (place_ref, col_keys.at[a, 1]),
            (emb_ref, cols.at[a]))[k]
        return pltpu.make_async_remote_copy(
            src_ref=src, dst_ref=dst, send_sem=col_send.at[b, k], recv_sem=col_recv.at[a, k],
            device_id={"blk": b}, device_id_type=MESH)

    def row_copy(e, k):
        src, dst = (
            (clusters_ref, row_keys.at[e, 0]), (place_ref, row_keys.at[e, 1]),
            (emb_ref, rows.at[pl.ds(e * n_rows, n_rows)]))[k]
        return pltpu.make_async_remote_copy(
            src_ref=src, dst_ref=dst, send_sem=row_send.at[e, k], recv_sem=row_recv.at[e, k],
            device_id={"owner": lax.rem(x + e, n_own)}, device_id_type=MESH)

    def col_return(a, b):
        return pltpu.make_async_remote_copy(
            src_ref=col_answer.at[a], dst_ref=col_back.at[b],
            send_sem=col_back_send.at[a], recv_sem=col_back_recv.at[b],
            device_id={"blk": a}, device_id_type=MESH)

    def row_return(e):
        return pltpu.make_async_remote_copy(
            src_ref=answer.at[e], dst_ref=row_back.at[e],
            send_sem=row_back_send.at[e], recv_sem=row_back_recv.at[e],
            device_id={"owner": lax.rem(x + n_own - e, n_own)}, device_id_type=MESH)

    def down(key):
        return jnp.transpose(jnp.broadcast_to(key, (n_rows, n_rows)))

    def unit(block):
        values = block.astype(jnp.float32)
        mean = jnp.mean(values * values, axis=1, keepdims=True)
        scaled = values * (lax.rsqrt(mean + 1e-06) * (1.0 / math.sqrt(width)))
        return scaled.astype(jnp.bfloat16)

    def send_cols(b):
        @pl.when(flows(z, b))
        def _():
            for k in range(3):
                col_copy(z, b, k).start()

    def send_rows(e):
        for k in range(3):
            row_copy(e, k).start()

    def key_of(clusters, place):
        return div_rem(place, cap, n_own) * 65536 + clusters

    targets = sum(flows(z, b).astype(jnp.int32) for b in range(n_blk))
    pl.semaphore_wait(barrier, targets + n_own - 1)
    each(0, n_blk, send_cols)
    each(1, n_own, send_rows)

    for load in loads:
        load.wait()
    my_key = key_of(row_keys[0, 0], row_keys[0, 1])
    rows[pl.ds(0, n_rows)] = unit(emb[...])

    def top(found):
        return jnp.max(found, axis=0, keepdims=True)

    mine = rows[pl.ds(0, n_rows)]
    shape = (n_rows, n_rows)
    other = lax.broadcasted_iota(jnp.int32, shape, 0) != lax.broadcasted_iota(jnp.int32, shape, 1)
    answer[...] = jnp.full(answer.shape, LOWEST, jnp.float32)
    answer[0] = top(jnp.where((down(my_key) == my_key) & other, pair_scores(mine, mine), LOWEST))

    def meet_row(e):
        for k in range(3):
            row_copy(e, k).wait_recv()
        theirs = unit(rows[pl.ds(e * n_rows, n_rows)])
        rows[pl.ds(e * n_rows, n_rows)] = theirs
        found = jnp.where(down(key_of(row_keys[e, 0], row_keys[e, 1])) == my_key, pair_scores(theirs, mine), LOWEST)
        answer[0] = jnp.maximum(answer[0], top(found))

    each(1, n_own, meet_row)

    last = functools.reduce(
        jnp.maximum, [jnp.where(flows(a, z), a, -1) for a in range(n_blk)])

    def meet_col(a):
        @pl.when(flows(a, z))
        def _():
            for k in range(2):
                col_copy(a, z, k).wait_recv()
            col_down = down(key_of(col_keys[a, 0], col_keys[a, 1]))
            col_copy(a, z, 2).wait_recv()
            scores = pair_scores(unit(cols[a]), rows[...])
            best = None
            for e in range(n_own):
                found = jnp.where(
                    col_down == key_of(row_keys[e, 0], row_keys[e, 1]), scores[:, e * n_rows:(e + 1) * n_rows], LOWEST)
                answer[e] = jnp.maximum(answer[e], top(found))
                best = found if best is None else jnp.maximum(best, found)

            @pl.when(a == last)
            def _():
                each(1, n_own, lambda e: row_return(e).start())

            col_answer[a] = top(jnp.transpose(best))
            col_return(a, z).start()

    each(0, n_blk, meet_col)

    @pl.when(last < 0)
    def _():
        each(1, n_own, lambda e: row_return(e).start())

    out_ref[...] = answer[0]

    def take_col(b):
        @pl.when(flows(z, b))
        def _():
            for k in range(3):
                col_copy(z, b, k).wait_send()
            col_return(z, b).wait_recv()
            out_ref[...] = jnp.maximum(out_ref[...], col_back[b])

        @pl.when(flows(b, z))
        def _():
            col_return(b, z).wait_send()

    def take_row(e):
        for k in range(3):
            row_copy(e, k).wait_send()
        row_return(e).wait()
        out_ref[...] = jnp.maximum(out_ref[...], row_back[e])

    each(0, n_blk, take_col)
    each(1, n_own, take_row)


def body(embeddings, clusters, place):
    n_rows, width = embeddings.shape
    n_blk = lax.axis_size("blk")
    n_own = lax.axis_size("owner")
    cap = 2 * n_rows // (n_blk * n_own)
    vmem = pl.BlockSpec(memory_space=pltpu.VMEM)
    dma = pltpu.SemaphoreType.DMA
    best = pl.pallas_call(
        functools.partial(kernel, n_blk, n_own, cap),
        out_shape=pltpu.VMEM((1, n_rows), jnp.float32),
        in_specs=[pl.BlockSpec(memory_space=pltpu.HBM)] * 3,
        out_specs=vmem,
        scratch_shapes=[
            pltpu.VMEM((n_rows, width), jnp.bfloat16),
            pltpu.VMEM((n_own * n_rows, width), jnp.bfloat16),
            pltpu.VMEM((n_own, 2, 1, n_rows), jnp.int32),
            pltpu.VMEM((n_blk, n_rows, width), jnp.bfloat16),
            pltpu.VMEM((n_blk, 2, 1, n_rows), jnp.int32),
            pltpu.VMEM((n_own, 1, n_rows), jnp.float32),
            pltpu.VMEM((n_blk, 1, n_rows), jnp.float32),
            pltpu.VMEM((n_blk, 1, n_rows), jnp.float32),
            pltpu.VMEM((n_own, 1, n_rows), jnp.float32),
            dma((3,)),
            dma((n_blk, 3)), dma((n_blk, 3)), dma((n_own, 3)), dma((n_own, 3)),
            dma((n_blk,)), dma((n_blk,)), dma((n_own,)), dma((n_own,)),
        ],
        compiler_params=pltpu.CompilerParams(collective_id=0, has_side_effects=True),
    )(embeddings, clusters.reshape(1, n_rows), place.reshape(1, n_rows))
    return best.reshape(n_rows)


def solution(mesh):
    spread = ("parts", "blk", "owner", "sub")
    return jax.shard_map(
        body, mesh=mesh, in_specs=(P(spread, None), P(spread), P(spread)), out_specs=P(spread),
        check_vma=False)
```

time: 15.4 us -> 14.6 us (0.948)
  Pallas kernels: 14.8 us -> 14 us
    pallas_call x1, Pallas kernels: 14.8 us -> 14 us  [body(): pl.pallas_call(functools.partial(kernel, n_blk, n_own, cap), out_shape=pl...]
where the time goes in v3:
time: 14.6 us; the launch traced here: 14.5 us
  Pallas kernels  14 us (96%)
  local copies, waits for them, and re-layouts  0.51 us (3%)
    pallas_call x1, Pallas kernels, body(): pl.pallas_call(functools.partial(kernel, n_blk, n_own, cap), out_shape=pl...  14 us
    unnamed x1, local copies, waits for them, and re-layouts  0.51 us

profile of v3, /device:TPU:0, one launch (start us, length us, event | category | flops | bytes accessed | tf_op | source)
XLA Modules:
  0.0 14.5 jit_solution(8390236578981826994)
XLA Ops:
  0.0 14.0 %shard_map.37 = f32[1,128]{1,0:T(1,128)S(1)} custom-call(bf16[128,512]{1,0:T(8,128)(2,1)} %emb_ref.1, s32[1,128]{1,0:T(1,128)} %bitcast.4, s32[1,128]{1,0:T(1,128)} %bitcast.5), custom_call_target="tpu_custom_call" | custom-call | tf_op jit(solution)/shard_map/pallas_call | solution.py:211
  14.0 0.5 %copy.5 = f32[128]{0:T(128)} copy(f32[128]{0:T(128)S(1)} %bitcast.3) | data formatting | bytes 1024

commit v4 on v3

--- a/solution.py
+++ b/solution.py
@@ -45,7 +45,8 @@
 
     def flows(a, b):
         low, apart = jnp.minimum(a, b), jnp.abs(a - b)
-        up = (apart < n_blk - 1) & ((sub == 0) | ((low == 1) & (apart == 1)))
+        up = (apart < n_blk - 1) & jnp.where(
+            sub == 0, (low == 0) | (apart == 2), (low == 1) & (apart == 1))
         return ((a < b) & up) | ((a > b) & ~up)
 
     loads = [
@@ -53,8 +54,6 @@
         for k, (src, dst) in enumerate((
             (emb_ref, emb), (clusters_ref, row_keys.at[0, 0]), (place_ref, row_keys.at[0, 1])))
     ]
-    for load in loads:
-        load.start()
 
     barrier = pltpu.get_barrier_semaphore()
     each(1, n_own, lambda e: pl.semaphore_signal(
@@ -121,6 +120,8 @@
     pl.semaphore_wait(barrier, targets + n_own - 1)
     each(0, n_blk, send_cols)
     each(1, n_own, send_rows)
+    for load in loads:
+        load.start()
 
     for load in loads:
         load.wait()

time: 14.6 us -> 14.6 us (level)
  no operation moved by 1% of the time
where the time goes in v4:
time: 14.6 us; the launch traced here: 14.5 us
  Pallas kernels  14 us (96%)
  local copies, waits for them, and re-layouts  0.51 us (3%)
    pallas_call x1, Pallas kernels, body(): pl.pallas_call(functools.partial(kernel, n_blk, n_own, cap), out_shape=pl...  14 us
    unnamed x1, local copies, waits for them, and re-layouts  0.51 us

profile of v4, /device:TPU:0, one launch (start us, length us, event | category | flops | bytes accessed | tf_op | source)
XLA Modules:
  0.0 14.5 jit_solution(918258399556315415)
XLA Ops:
  0.0 14.0 %shard_map.37 = f32[1,128]{1,0:T(1,128)S(1)} custom-call(bf16[128,512]{1,0:T(8,128)(2,1)} %emb_ref.1, s32[1,128]{1,0:T(1,128)} %bitcast.4, s32[1,128]{1,0:T(1,128)} %bitcast.5), custom_call_target="tpu_custom_call" | custom-call | tf_op jit(solution)/shard_map/pallas_call | solution.py:212
  14.0 0.5 %copy.5 = f32[128]{0:T(128)} copy(f32[128]{0:T(128)S(1)} %bitcast.3) | data formatting | bytes 1024
